TPU v7x, 256 devices: a whole 4x4x8 slice. The times are simulated.
256 devices in a mesh: sub: 64 (over z, x, core), face: 4 (over y).
Axes of the slice: x: 4, y: 4, z: 8, core: 2. Of those that a mesh axis runs over, the one named last changes fastest.
Arguments:
- own_block: bfloat16 [1024, 512, 512], P(('sub', 'face')), may hold values from -1 to 4, as said below
- own_coupling: bfloat16 [1024, 512, 512], P(('sub', 'face')), may hold values from -0.125 to 0.125
- lent_block: bfloat16 [1024, 512, 512], P(('sub', 'face')), may hold values from -1 to 4, as said below
- lent_coupling: bfloat16 [1024, 512, 512], P(('sub', 'face')), may hold values from -0.125 to 0.125
- face_list: int32 [1024, 2], replicated, may hold values from 0 to 63, as said below
- eig_counts: int32 [1024], P('sub'), may hold values from 1 to 32, as said below
- owner_map: int32 [1024, 1], replicated, may hold values from 0 to 63, as said below
- start_block: float32 [1024, 32, 512], P('sub', None, 'face'), may hold values from -6 to 6
Outputs:
- basis_rows: float32 [1024, 32, 512], P('sub', None, 'face')
- coarse: float32 [1024, 1024], P('sub', 'face')
Inputs may be any that keep to these rules, and one draw needn't show every extreme that they name: `face_list`: face f, held by subdomain i = f // 16, pairs with subdomain (i + d) mod 64 for a distance d of 1 to 4; every lent slot of every subdomain is named by exactly one face; the lent slot lies in the same group of 4 slots as the face's own slot (f mod 16) // 4; every subdomain has the same number of faces at each distance, one distance holds exactly 8 of them and no distance more, and some face has distance 4. `eig_counts`: the counts 1 and 32 both occur. `owner_map`: face f of subdomain s = f // 16 has owner (s + d * 16) mod 64 for some d from 0 to 3, and exactly 4 faces of s have each of these 4 owners. `own_block`: symmetric; diagonal entries between 2 and 4. `lent_block`: symmetric; diagonal entries between 2 and 4.
All inputs are finite; a program needn't handle non-finite values.
Results may differ from a plain program's by a relative error of at most 0.0049.
Values may be sent and summed in bfloat16 or wider, within the bound.
A program may use at most 192 MiB of HBM per device.

v0:
```python
import jax
import jax.numpy as jnp
from jax import lax
from jax.sharding import PartitionSpec as P

ITERS = 3
REACH = 4


HIGHEST = lax.Precision.HIGHEST


def shifted(block, axis, distance):
    devices = range(lax.axis_size(axis))
    route = [((i - distance) % len(devices), i) for i in devices]
    return lax.ppermute(block, axis, route)


def face_schur(face_block, coupling):
    product = jnp.einsum("fin,fim->fnm", coupling, coupling, preferred_element_type=jnp.float32)
    schur = (face_block.astype(jnp.float32) - product).astype(jnp.bfloat16)
    return (schur, jnp.diagonal(face_block, axis1=1, axis2=2))


def apply_rows(iterate, operator):
    return jnp.einsum("fkm,frm->fkr", iterate, operator, precision=HIGHEST)


def full_iterate(piece):
    return lax.all_gather(piece, "face", axis=2, tiled=True)


def route_lent(held_rows, held_weight, lent_rows, lent_weight, face_list, face_count, first_slot):
    sub_count = lax.axis_size("sub")
    my_sub = lax.axis_index("sub")
    local_count = held_rows.shape[0]
    partners = face_list[:, 0]
    partner_slots = face_list[:, 1]
    homes = jnp.arange(face_list.shape[0], dtype=jnp.int32) // face_count
    distances = (partners - homes) % sub_count
    my_distance = lax.dynamic_slice_in_dim(
        distances, my_sub * face_count + first_slot, local_count, 0
    )
    my_slots = (
        lax.dynamic_slice_in_dim(partner_slots, my_sub * face_count + first_slot, local_count, 0)
        - first_slot
    )
    local_range = jnp.arange(local_count, dtype=jnp.int32)
    gathered_rows = jnp.zeros(held_rows.shape, jnp.float32)
    gathered_weight = jnp.zeros(held_weight.shape, jnp.float32)
    for distance in range(1, REACH + 1):
        got_rows, got_weight = shifted((lent_rows, lent_weight), "sub", -distance)
        chooser = (
            (my_distance == distance)[:, None] & (my_slots[:, None] == local_range[None, :])
        ).astype(jnp.bfloat16)
        gathered_rows = gathered_rows + jnp.einsum(
            "sq,qrn->srn", chooser, got_rows, preferred_element_type=jnp.float32
        )
        gathered_weight = gathered_weight + jnp.einsum(
            "sq,qr->sr", chooser, got_weight, preferred_element_type=jnp.float32
        )
    operator = held_rows.astype(jnp.float32) + gathered_rows
    weight = held_weight.astype(jnp.float32) + gathered_weight
    return (operator, weight)


def shards(
    own_block,
    own_coupling,
    lent_block,
    lent_coupling,
    face_list,
    eig_counts,
    owner_map,
    start_block,
):
    my_sub = lax.axis_index("sub")
    my_part = lax.axis_index("face")
    face_count = eig_counts.shape[0]
    block_size = start_block.shape[1]
    own_schur, own_diagonal = face_schur(own_block, own_coupling)
    lent_schur, lent_diagonal = face_schur(lent_block, lent_coupling)
    own_rows, own_weight, lent_rows, lent_weight = (
        lax.all_to_all(own_schur, "face", split_axis=1, concat_axis=0, tiled=True),
        lax.all_to_all(own_diagonal, "face", split_axis=1, concat_axis=0, tiled=True),
        lax.all_to_all(lent_schur, "face", split_axis=1, concat_axis=0, tiled=True),
        lax.all_to_all(lent_diagonal, "face", split_axis=1, concat_axis=0, tiled=True),
    )
    operator, weight = route_lent(
        own_rows, own_weight, lent_rows, lent_weight, face_list, face_count, 0
    )
    iterate = start_block
    for sweep_index in range(ITERS):
        whole = full_iterate(iterate)
        image_part = apply_rows(whole, operator) / weight[:, None, :]
        partial_gram = jnp.einsum(
            "fkr,flr->fkl", image_part * weight[:, None, :], image_part, precision=HIGHEST
        )
        gram_matrix = lax.psum(partial_gram, "face")
        lower_factor = jnp.linalg.cholesky(gram_matrix)
        iterate = jax.scipy.linalg.solve_triangular(lower_factor, image_part, lower=True)
    whole = full_iterate(iterate)
    applied = apply_rows(whole, operator)
    terms = jnp.einsum("fkr,flr->fkl", iterate, applied, precision=HIGHEST).reshape(
        face_count, block_size * block_size
    )
    quarter = lax.psum_scatter(terms, "face", scatter_dimension=1, tiled=True)
    part_width = quarter.shape[1]
    kept = (jnp.arange(block_size, dtype=jnp.int32)[None, :] < eig_counts[:, None]).astype(
        jnp.float32
    )
    basis_rows = iterate * kept[:, :, None]
    kept_pairs = (kept[:, :, None] * kept[:, None, :]).reshape(face_count, block_size * block_size)
    kept_part = lax.dynamic_slice_in_dim(kept_pairs, my_part * part_width, part_width, 1)
    owned_blocks = quarter * kept_part
    owners = owner_map[:, 0]
    row_range = jnp.arange(face_count, dtype=jnp.int32)
    every_block = lax.all_gather(owned_blocks, "sub", axis=0, tiled=True)
    wanted = owners == my_sub
    rank_among = jnp.cumsum(wanted.astype(jnp.int32)) - 1
    placer = (wanted[None, :] & (rank_among[None, :] == row_range[:, None])).astype(jnp.float32)
    coarse = jnp.dot(placer, every_block, precision=HIGHEST)
    return (basis_rows, coarse)


def solution(mesh):
    placed = (
        P(("sub", "face"), None, None),
        P(("sub", "face"), None, None),
        P(("sub", "face"), None, None),
        P(("sub", "face"), None, None),
        P(),
        P("sub"),
        P(),
        P("sub", None, "face"),
    )
    return jax.shard_map(
        shards,
        mesh=mesh,
        in_specs=placed,
        out_specs=(P("sub", None, "face"), P("sub", "face")),
        check_vma=False,
    )
```

profile of v0, /device:TPU:1, one launch (start us, length us, event | category | flops | bytes accessed | tf_op | source)
XLA Modules:
  0.0 978.9 jit_solution(8873128093800474863)
XLA Ops:
  20.5 43.0 %copy.75 = bf16[4,512,512]{0,2,1:T(8,128)(2,1)} copy(bf16[4,512,512]{2,1,0:T(8,128)(2,1)S(1)} %copy-done.3) | data formatting | bytes 4194304 | tf_op args[0]
  80.7 44.1 %copy.77 = bf16[4,512,512]{0,2,1:T(8,128)(2,1)} copy(bf16[4,512,512]{2,1,0:T(8,128)(2,1)} %param.13) | data formatting | bytes 4194304 | tf_op args[2]
  136.9 8.9 collective-permute-start.2
  165.1 26.7 %collective-permute-done.7 = bf16[16,128]{1,0:T(8,128)(2,1)S(1)} collective-permute-done((bf16[16,128]{1,0:T(8,128)(2,1)S(1)}, bf16[16,128]{1,0:T(8,128)(2,1)S(1)}, u32[]{:S(2)}, u32[]{:S(2)}) %collective-permute-start.7) | collective-permute-done | bytes 4128 | tf_op jit(solution)/shard_map/ppermute | solution.py:16
  192.3 44.5 %collective-permute-done.6 = bf16[16,128]{1,0:T(8,128)(2,1)S(1)} collective-permute-done((bf16[16,128]{1,0:T(8,128)(2,1)S(1)}, bf16[16,128]{1,0:T(8,128)(2,1)S(1)}, u32[]{:S(2)}, u32[]{:S(2)}) %collective-permute-start.6) | collective-permute-done | bytes 4128 | tf_op jit(solution)/shard_map/ppermute | solution.py:16
  236.8 28.6 %collective-permute-start.3 = (bf16[16,128,512]{2,0,1:T(8,128)(2,1)}, bf16[16,128,512]{2,0,1:T(8,128)(2,1)}, u32[]{:S(2)}, u32[]{:S(2)}) collective-permute-start(bf16[16,128,512]{2,0,1:T(8,128)(2,1)} %all_to_all.48), channel_id=1, source_target_pairs={{16,0},{20,4},{24,8},{28,12},{32,16},{36,20},{40,24},{44,28},{48,3... | collective-permute-start | bytes 6291464 | tf_op jit(solution)/shard_map/ppermute | solution.py:16
  285.5 20.8 %collective-permute-done.3 = bf16[16,128,512]{2,0,1:T(8,128)(2,1)} collective-permute-done((bf16[16,128,512]{2,0,1:T(8,128)(2,1)}, bf16[16,128,512]{2,0,1:T(8,128)(2,1)}, u32[]{:S(2)}, u32[]{:S(2)}) %collective-permute-start.3) | collective-permute-done | bytes 2097184 | tf_op jit(solution)/shard_map/ppermute | solution.py:16
  311.1 8.6 fusion.6
  321.1 59.6 %all-reduce.4.cloned.1.call-done = f32[16,32,32]{1,2,0:T(8,128)} async-done(((f32[16,32,32]{1,2,0:T(8,128)}), f32[16,32,32]{1,2,0:T(8,128)}) %all-reduce.4.cloned.1.call-update) | async-done | bytes 65552 | tf_op jit(solution)/shard_map/psum | solution.py:99
  382.7 46.9 %custom-call.14 = f32[16,32,32]{2,1,0:T(8,128)S(1)} custom-call(f32[16,32,32]{2,1,0:T(8,128)S(1)} %fusion.29), custom_call_target="Cholesky" | custom-call | tf_op jit(solution)/shard_map/jit(cholesky)/cholesky | solution.py:100
  429.9 39.4 %custom-call.15 = f32[16,1,32,32]{2,3,1,0:T(8,128)S(1)} custom-call(f32[16,1,32,32]{3,2,1,0:T(8,128)S(1)} %select_bitcast_fusion.2), custom_call_target="InvertDiagBlocksLowerTriangular" | custom-call | tf_op jit(solution)/shard_map/jit(_solve_triangular)/vmap()/triangular_solve | solution.py:101
  470.9 30.1 %all-gather.8.cloned.1.call-done = f32[16,32,512]{2,1,0:T(8,128)} async-done(((f32[16,32,128]{2,1,0:T(8,128)}), f32[16,32,512]{2,1,0:T(8,128)}) %all-gather.8.cloned.1.call-update) | async-done | bytes 1048592 | tf_op jit(solution)/shard_map/all_gather | solution.py:30
  501.0 8.6 fusion.8
  510.9 46.6 %all-reduce.6.cloned.1.call-done = f32[16,32,32]{1,2,0:T(8,128)} async-done(((f32[16,32,32]{1,2,0:T(8,128)}), f32[16,32,32]{1,2,0:T(8,128)}) %all-reduce.6.cloned.1.call-update) | async-done | bytes 65552 | tf_op jit(solution)/shard_map/psum | solution.py:99
  559.6 46.9 %custom-call.16 = f32[16,32,32]{2,1,0:T(8,128)S(1)} custom-call(f32[16,32,32]{2,1,0:T(8,128)S(1)} %fusion.26), custom_call_target="Cholesky" | custom-call | tf_op jit(solution)/shard_map/jit(cholesky)/cholesky | solution.py:100
  606.8 39.4 %custom-call.17 = f32[16,1,32,32]{2,3,1,0:T(8,128)S(1)} custom-call(f32[16,1,32,32]{3,2,1,0:T(8,128)S(1)} %select_bitcast_fusion.1), custom_call_target="InvertDiagBlocksLowerTriangular" | custom-call | tf_op jit(solution)/shard_map/jit(_solve_triangular)/vmap()/triangular_solve | solution.py:101
  647.8 30.0 %all-gather.10.cloned.1.call-done = f32[16,32,512]{2,1,0:T(8,128)} async-done(((f32[16,32,128]{2,1,0:T(8,128)}), f32[16,32,512]{2,1,0:T(8,128)}) %all-gather.10.cloned.1.call-update) | async-done | bytes 1048592 | tf_op jit(solution)/shard_map/all_gather | solution.py:30
  677.9 8.6 fusion.11
  687.9 46.6 %all-reduce.8.cloned.1.call-done = f32[16,32,32]{1,2,0:T(8,128)} async-done(((f32[16,32,32]{1,2,0:T(8,128)}), f32[16,32,32]{1,2,0:T(8,128)}) %all-reduce.8.cloned.1.call-update) | async-done | bytes 65552 | tf_op jit(solution)/shard_map/psum | solution.py:99
  736.5 46.9 %custom-call.18 = f32[16,32,32]{2,1,0:T(8,128)S(1)} custom-call(f32[16,32,32]{2,1,0:T(8,128)S(1)} %fusion.23), custom_call_target="Cholesky" | custom-call | tf_op jit(solution)/shard_map/jit(cholesky)/cholesky | solution.py:100
  783.7 39.4 %custom-call.19 = f32[16,1,32,32]{2,3,1,0:T(8,128)S(1)} custom-call(f32[16,1,32,32]{3,2,1,0:T(8,128)S(1)} %select_bitcast_fusion), custom_call_target="InvertDiagBlocksLowerTriangular" | custom-call | tf_op jit(solution)/shard_map/jit(_solve_triangular)/vmap()/triangular_solve | solution.py:101
  824.9 30.0 %all-gather.12.cloned.1.call-done = f32[16,32,512]{2,1,0:T(8,128)} async-done(((f32[16,32,128]{2,1,0:T(8,128)}), f32[16,32,512]{2,1,0:T(8,128)}) %all-gather.12.cloned.1.call-update) | async-done | bytes 1048592 | tf_op jit(solution)/shard_map/all_gather | solution.py:30
  865.1 22.4 %reduce-scatter.2.cloned.1.call-done = f32[16,256]{1,0:T(8,128)} async-done(((f32[16,1024]{1,0:T(8,128)}), f32[16,256]{1,0:T(8,128)}) %reduce-scatter.2.cloned.1.call-update) | async-done | bytes 16400 | tf_op jit(solution)/shard_map/reduce_scatter | solution.py:107
  889.5 80.1 %all-gather.14.cloned.1.call-done = f32[1024,256]{1,0:T(8,128)} async-done(((f32[16,256]{1,0:T(8,128)}), f32[1024,256]{1,0:T(8,128)}) %all-gather.14.cloned.1.call-update) | async-done | bytes 1048592 | tf_op jit(solution)/shard_map/all_gather | solution.py:118
  (118 shorter events, 117.5 us)
Async XLA Ops:
  14.7 55.9 %all-to-all-start.1 = ((bf16[4,512,512]{2,0,1:T(4,128)(2,1)}), bf16[4,512,512]{2,0,1:T(4,128)(2,1)}, u32[]{:S(2)}, u32[]{:S(2)}) async-start(bf16[4,512,512]{2,0,1:T(4,128)(2,1)} %copy.72), calls=%async_computation.1 | async-start | bytes 4194304 | tf_op jit(solution)/shard_map/all_to_all | solution.py:86
  19.7 291.4 %all-gather.6.cloned.1.call-start = ((), (), s32[]{:S(2)}) async-start(), calls=%async_computation.5 | async-start | bytes 1310720 | tf_op jit(solution)/shard_map/all_gather | solution.py:30
  70.6 75.2 %all-to-all-start.2 = ((bf16[4,4,128]{2,0,1:T(4,128)(2,1)}), bf16[4,4,128]{2,0,1:T(4,128)(2,1)S(1)}, u32[]{:S(2)}, u32[]{:S(2)}) async-start(bf16[4,4,128]{2,0,1:T(4,128)(2,1)} %copy.76), calls=%async_computation.2 | async-start | bytes 8192 | tf_op jit(solution)/shard_map/all_to_all | solution.py:85
  136.9 141.4 %collective-permute-start.2 = (bf16[16,128,512]{2,0,1:T(8,128)(2,1)}, bf16[16,128,512]{2,0,1:T(8,128)(2,1)}, u32[]{:S(2)}, u32[]{:S(2)}) collective-permute-start(bf16[16,128,512]{2,0,1:T(8,128)(2,1)} %all_to_all.48), channel_id=1, source_target_pairs={{12,0},{16,4},{20,8},{24,12},{28,16},{32,20},{36,24},{40,28},{44,3... | collective-permute-start | bytes 6291464 | tf_op jit(solution)/shard_map/ppermute | solution.py:16
  145.8 9.1 all-to-all-start.3
  154.9 114.9 %all-to-all-start = ((bf16[4,512,512]{2,0,1:T(4,128)(2,1)}), bf16[4,512,512]{2,0,1:T(4,128)(2,1)S(1)}, u32[]{:S(2)}, u32[]{:S(2)}) async-start(bf16[4,512,512]{2,0,1:T(4,128)(2,1)} %copy.69), calls=%async_computation | async-start | bytes 4194304 | tf_op jit(solution)/shard_map/all_to_all | solution.py:84
  159.1 221.5 %all-reduce.4.cloned.1.call-start = ((), (), s32[]{:S(2)}) async-start(), calls=%async_computation.6 | async-start | bytes 524288 | tf_op jit(solution)/shard_map/psum | solution.py:99
  159.2 121.5 %collective-permute-start = (bf16[16,128,512]{2,0,1:T(8,128)(2,1)}, bf16[16,128,512]{2,0,1:T(8,128)(2,1)}, u32[]{:S(2)}, u32[]{:S(2)}) collective-permute-start(bf16[16,128,512]{2,0,1:T(8,128)(2,1)} %all_to_all.48), channel_id=1, source_target_pairs={{4,0},{8,4},{12,8},{16,12},{20,16},{24,20},{28,24},{32,28},{36,32}... | collective-permute-start | bytes 6291464 | tf_op jit(solution)/shard_map/ppermute | solution.py:16
  159.4 32.4 %collective-permute-start.7 = (bf16[16,128]{1,0:T(8,128)(2,1)S(1)}, bf16[16,128]{1,0:T(8,128)(2,1)S(1)}, u32[]{:S(2)}, u32[]{:S(2)}) collective-permute-start(bf16[16,128]{1,0:T(8,128)(2,1)S(1)} %bitcast.111), channel_id=1, source_target_pairs={{16,0},{20,4},{24,8},{28,12},{32,16},{36,20},{40,24},{44,28},{48,3... | collective-permute-start | bytes 12296 | tf_op jit(solution)/shard_map/ppermute | solution.py:16
  161.1 121.9 %collective-permute-start.1 = (bf16[16,128,512]{2,0,1:T(8,128)(2,1)}, bf16[16,128,512]{2,0,1:T(8,128)(2,1)}, u32[]{:S(2)}, u32[]{:S(2)}) collective-permute-start(bf16[16,128,512]{2,0,1:T(8,128)(2,1)} %all_to_all.48), channel_id=1, source_target_pairs={{8,0},{12,4},{16,8},{20,12},{24,16},{28,20},{32,24},{36,28},{40,32... | collective-permute-start | bytes 6291464 | tf_op jit(solution)/shard_map/ppermute | solution.py:16
  163.2 73.6 %collective-permute-start.6 = (bf16[16,128]{1,0:T(8,128)(2,1)S(1)}, bf16[16,128]{1,0:T(8,128)(2,1)S(1)}, u32[]{:S(2)}, u32[]{:S(2)}) collective-permute-start(bf16[16,128]{1,0:T(8,128)(2,1)S(1)} %bitcast.112), channel_id=1, source_target_pairs={{12,0},{16,4},{20,8},{24,12},{28,16},{32,20},{36,24},{40,28},{44,3... | collective-permute-start | bytes 12296 | tf_op jit(solution)/shard_map/ppermute | solution.py:16
  191.8 73.9 %collective-permute-start.5 = (bf16[16,128]{1,0:T(8,128)(2,1)S(1)}, bf16[16,128]{1,0:T(8,128)(2,1)S(1)}, u32[]{:S(2)}, u32[]{:S(2)}) collective-permute-start(bf16[16,128]{1,0:T(8,128)(2,1)S(1)} %bitcast.113), channel_id=1, source_target_pairs={{8,0},{12,4},{16,8},{20,12},{24,16},{28,20},{32,24},{36,28},{40,32... | collective-permute-start | bytes 12296 | tf_op jit(solution)/shard_map/ppermute | solution.py:16
  236.8 69.6 %collective-permute-start.3 = (bf16[16,128,512]{2,0,1:T(8,128)(2,1)}, bf16[16,128,512]{2,0,1:T(8,128)(2,1)}, u32[]{:S(2)}, u32[]{:S(2)}) collective-permute-start(bf16[16,128,512]{2,0,1:T(8,128)(2,1)} %all_to_all.48), channel_id=1, source_target_pairs={{16,0},{20,4},{24,8},{28,12},{32,16},{36,20},{40,24},{44,28},{48,3... | collective-permute-start | bytes 6291464 | tf_op jit(solution)/shard_map/ppermute | solution.py:16
  265.6 4.0 collective-permute-start.4
  321.0 180.0 %all-gather.8.cloned.1.call-start = ((), (), s32[]{:S(2)}) async-start(), calls=%async_computation.7 | async-start | bytes 1310720 | tf_op jit(solution)/shard_map/all_gather | solution.py:30
  470.7 86.9 %all-reduce.6.cloned.1.call-start = ((), (), s32[]{:S(2)}) async-start(), calls=%async_computation.8 | async-start | bytes 524288 | tf_op jit(solution)/shard_map/psum | solution.py:99
  510.9 167.0 %all-gather.10.cloned.1.call-start = ((), (), s32[]{:S(2)}) async-start(), calls=%async_computation.9 | async-start | bytes 1310720 | tf_op jit(solution)/shard_map/all_gather | solution.py:30
  606.5 81.3 %copy-start.7 = (s32[16]{0:T(128)S(1)}, s32[16]{0:T(128)}, u32[]{:S(2)}) copy-start(s32[16]{0:T(128)} %param.16) | copy-start | bytes 196
  647.5 86.9 %all-reduce.8.cloned.1.call-start = ((), (), s32[]{:S(2)}) async-start(), calls=%async_computation.10 | async-start | bytes 524288 | tf_op jit(solution)/shard_map/psum | solution.py:99
  687.7 167.1 %all-gather.12.cloned.1.call-start = ((), (), s32[]{:S(2)}) async-start(), calls=%async_computation.11 | async-start | bytes 1310720 | tf_op jit(solution)/shard_map/all_gather | solution.py:30
  823.1 65.8 %copy-start.6 = (s32[1024,1]{0,1:T(1,128)S(1)}, s32[1024,1]{0,1:T(1,128)}, u32[]{:S(2)}) copy-start(s32[1024,1]{0,1:T(1,128)} %param.17) | copy-start | bytes 12292
  824.6 62.9 %reduce-scatter.2.cloned.1.call-start = ((), (), s32[]{:S(2)}) async-start(), calls=%async_computation.12 | async-start | bytes 81920 | tf_op jit(solution)/shard_map/reduce_scatter | solution.py:107
  824.9 147.0 %copy-start.1 = (bf16[4,512,512]{2,1,0:T(8,128)(2,1)S(1)}, bf16[4,512,512]{2,1,0:T(8,128)(2,1)}, u32[]{:S(2)}) copy-start(bf16[4,512,512]{2,1,0:T(8,128)(2,1)} %param.14) | copy-start | bytes 6291460
  864.8 104.7 %all-gather.14.cloned.1.call-start = ((), (), s32[]{:S(2)}) async-start(), calls=%async_computation.13 | async-start | bytes 1064960 | tf_op jit(solution)/shard_map/all_gather | solution.py:118
  (5 other events, 91.0 us)
Sparse Core Ops, SparseCore 0:
  22.3 35.2 all-gather.5
  321.1 59.4 all-reduce.3
  470.8 30.1 all-gather.7
  511.0 46.5 all-reduce.5
  647.7 30.1 all-gather.9
  687.9 46.5 all-reduce.7
  824.7 30.1 all-gather.11
  864.9 22.5 reduce-scatter.1
  890.8 78.6 all-gather.13
where the time goes:
time: 992 us; the launch traced here: 979 us
  waiting for transfers between devices  442 us (45%)
  other arithmetic  268 us (27%)
  local copies, waits for them, and re-layouts  125 us (13%)
  matrix products  66.2 us (7%)
  starting transfers between devices  63.1 us (6%)
  between operations  14.6 us (1%)
    psum x3, waiting for transfers between devices, shards(): gram_matrix = lax.psum(partial_gram, 'face')  153 us
    another operation x10, other arithmetic, shards(): lower_factor = jnp.linalg.cholesky(gram_matrix)  141 us
    another operation x7, other arithmetic, shards(): jax.scipy.linalg.solve_triangular(lower_factor, image_part, lower=True)  119 us
    ppermute x8, waiting for transfers between devices, shifted(): return lax.ppermute(block, axis, route)  95.7 us
    all_gather x4, waiting for transfers between devices, full_iterate(): return lax.all_gather(piece, 'face', axis=2, tiled=True)  90.1 us
    unnamed x18, local copies, waits for them, and re-layouts  88.8 us
    all_gather x1, waiting for transfers between devices, shards(): every_block = lax.all_gather(owned_blocks, 'sub', axis=0, tiled=True)  80.1 us
    ppermute x8, starting transfers between devices, shifted(): return lax.ppermute(block, axis, route)  43.8 us
  transfers between devices with their start and end apart: 21, of which 12 were waited for; matrix products, arithmetic and copies ran while one was open for 14% of the time, Pallas kernels for 0%

commit v1 on v0

v1 whole, which is shorter than its diff:
```python
import functools

import jax
import jax.numpy as jnp
from jax import lax
from jax.experimental import pallas as pl
from jax.experimental.pallas import tpu as pltpu
from jax.sharding import PartitionSpec as P

ITERS = 3
REACH = 4
RING = 4
PLUS = (0, 1)

HIGHEST = lax.Precision.HIGHEST
MESH = pl.DeviceIdType.MESH
F32 = jnp.float32
BF16 = jnp.bfloat16


def iota(shape, dim):
    return lax.broadcasted_iota(jnp.int32, shape, dim)


def dot(a, b, ca, cb, precision=None):
    return lax.dot_general(
        a, b, (((ca,), (cb,)), ((), ())), precision=precision, preferred_element_type=F32
    )


def pack_lent(block, coupling, out_ref):
    n = block.shape[0]
    h = n // 2
    c0, c1 = coupling[:, :h], coupling[:, h:]
    b00 = block[:h, :h].astype(F32)
    b11 = block[h:, h:].astype(F32)
    row, col = iota((h, h), 0), iota((h, h), 1)
    out_ref[0:h, :] = (block[:h, h:].astype(F32) - dot(c0, c1, 0, 0)).astype(BF16)
    s00 = b00 - dot(c0, c0, 0, 0)
    s11 = b11 - dot(c1, c1, 0, 0)
    out_ref[h : 2 * h, :] = jnp.where(row <= col, s00, s11).astype(BF16)
    eye = row == col
    diagonals = [jnp.sum(jnp.where(eye, v, 0.0), axis=0, keepdims=True) for v in (s11, b00, b11)]
    at = iota((16, h), 0)
    aux = jnp.where(at == 0, diagonals[0], jnp.where(at == 1, diagonals[1], diagonals[2]))
    out_ref[2 * h :, :] = aux.astype(BF16)


def unpack_lent(packed, out_ref):
    h = packed.shape[1]
    upper = packed[0:h]
    mixed = packed[h : 2 * h].astype(F32)
    aux = packed[2 * h :].astype(F32)
    flipped = mixed.T
    row, col = iota((h, h), 0), iota((h, h), 1)
    out_ref[:h, :h] = jnp.where(row <= col, mixed, flipped).astype(BF16)
    out_ref[h:, h:] = jnp.where(
        row > col, mixed, jnp.where(row < col, flipped, aux[0:1])
    ).astype(BF16)
    out_ref[:h, h:] = upper
    out_ref[h:, :h] = upper.astype(F32).T.astype(BF16)
    return jnp.concatenate([aux[1:2], aux[2:3]], axis=1)


def kernel(
    subs,
    parts,
    own_block,
    own_coupling,
    lent_block,
    lent_coupling,
    start_block,
    owners_ref,
    meta,
    basis,
    coarse,
    lent_b,
    lent_c,
    own_b,
    own_c,
    own_s,
    lent_s,
    tx,
    rx,
    passing,
    x0,
    basis_tx,
    cand_tx,
    cand,
    load_sem,
    x0_local_sem,
    lane1_send,
    lane1_recv,
    mid_send,
    mid_recv,
    lane2_send,
    lane2_recv,
    near_send,
    near_recv,
    far_send,
    far_recv,
    x0_send,
    x0_recv,
    basis_send,
    basis_recv,
    cand_send,
    cand_recv,
):
    faces = own_b.shape[0]
    n = own_b.shape[1]
    k = start_block.shape[1]
    width = start_block.shape[2]
    me = lax.axis_index("sub")
    part = lax.axis_index("face")
    core = lax.rem(me, 2)
    x = lax.rem(me // 2, RING)
    line = me - 2 * x - core
    ahead = line + 2 * lax.rem(x + 1, RING) + core
    behind = line + 2 * lax.rem(x + RING - 1, RING) + core
    spacing = subs // 4
    residue = lax.rem(me, spacing)
    turn = me // spacing

    def around(s):
        return lax.rem(s + 2 * subs, subs)

    other = me + 1 - 2 * core
    down = around(me - 2)
    up = around(me + 2)
    onward = around(behind - 4)
    top = around(me + 4)
    top_core = lax.rem(top, 2)
    top_x = lax.rem(top // 2, RING)
    feeder = top - 2 * top_x + 2 * lax.rem(top_x + 1, RING)

    loads = []
    for f in range(faces):
        for a, (src, dst) in enumerate(((lent_coupling, lent_c), (lent_block, lent_b))):
            loads.append(pltpu.make_async_copy(src.at[f], dst.at[f], load_sem.at[a, f]))
    for f in range(faces):
        for a, (src, dst) in enumerate(((own_coupling, own_c), (own_block, own_b))):
            loads.append(pltpu.make_async_copy(src.at[f], dst.at[f], load_sem.at[a + 2, f]))
    for copy in loads:
        copy.start()
    x0_local = pltpu.make_async_copy(
        start_block.at[pl.ds(part * faces, faces)], x0.at[part], x0_local_sem
    )
    x0_local.start()

    def remote(src, dst, send, recv, s, p):
        return pltpu.make_async_remote_copy(
            src_ref=src,
            dst_ref=dst,
            send_sem=send,
            recv_sem=recv,
            device_id=(s, p),
            device_id_type=MESH,
        )

    barrier = pltpu.get_barrier_semaphore()
    greeted = [(s, part) for s in (down, up, ahead, behind, onward, feeder, other)]
    peers = []
    for dk in range(4):
        for dp in range(parts):
            if dk or dp:
                s = residue + spacing * lax.rem(turn + dk, 4)
                p = lax.rem(part + dp, parts)
                peers.append((dk, dp, s, p))
                greeted.append((s, p))
    for s, p in greeted:
        pl.semaphore_signal(barrier, inc=1, device_id=(s, p), device_id_type=MESH)
    pl.semaphore_wait(barrier, len(greeted))

    x0_copies = []
    for dp in range(1, parts):
        p = lax.rem(part + dp, parts)
        x0_copies.append(
            remote(
                start_block.at[pl.ds(p * faces, faces)],
                x0.at[part],
                x0_send.at[dp - 1],
                x0_recv.at[dp - 1],
                me,
                p,
            )
        )
    lane1 = [
        remote(tx.at[f], rx.at[faces + f], lane1_send.at[f], lane1_recv.at[f], down, part)
        for f in range(faces)
    ]
    mid = [
        remote(tx.at[f], passing.at[i], mid_send.at[i], mid_recv.at[i], ahead, part)
        for i, f in enumerate(PLUS)
    ]
    lane2 = []
    for f in range(faces):
        if f in PLUS:
            src, s = passing.at[PLUS.index(f)], onward
        else:
            src, s = rx.at[faces + f], down
        lane2.append(
            remote(src, rx.at[3 * faces + f], lane2_send.at[f], lane2_recv.at[f], s, part)
        )

    def near(f, src):
        return remote(src, rx.at[f], near_send.at[f], near_recv.at[f], other, part)

    def far(f, src):
        return remote(src, rx.at[2 * faces + f], far_send.at[f], far_recv.at[f], other, part)

    for f in range(faces):
        loads[2 * f].wait()
        loads[2 * f + 1].wait()
        pack_lent(lent_b[f], lent_c[f], tx.at[f])
        lane1[f].start()
        if f in PLUS:
            mid[PLUS.index(f)].start()

        @pl.when(core == 1)
        def _():
            near(f, tx.at[f]).start()

    for copy in x0_copies:
        copy.start()

    own_weights = []
    eye = iota((n, n), 0) == iota((n, n), 1)
    for f in range(faces):
        loads[2 * faces + 2 * f].wait()
        loads[2 * faces + 2 * f + 1].wait()
        coupling = own_c[f]
        block = own_b[f].astype(F32)
        own_s[f] = (block - dot(coupling, coupling, 0, 0)).astype(BF16)
        own_weights.append(jnp.sum(jnp.where(eye, block, 0.0), axis=0, keepdims=True))
        lane1[f].wait_recv()
        if f not in PLUS:
            lane2[f].start()

        @pl.when(core == 0)
        def _():
            near(f, rx.at[faces + f]).start()

        @pl.when(core == 1)
        def _():
            far(f, rx.at[faces + f]).start()

        if f in PLUS:
            mid[PLUS.index(f)].wait_recv()
            lane2[f].start()

    x0_local.wait()
    for copy in x0_copies:
        copy.wait_recv()
    iterate = jnp.concatenate([x0[p].reshape(faces * k, width) for p in range(parts)], axis=1)

    def split(value):
        high = value.astype(BF16)
        return high, (value - high.astype(F32)).astype(BF16)

    def face_rows(value, f):
        return value[f * k : (f + 1) * k]

    def apply(value, tables):
        high, low = split(value)
        out = []
        for f in range(faces):
            stacked = jnp.concatenate([face_rows(high, f), face_rows(low, f)], axis=0)
            got = sum(dot(stacked, table[f], 1, 0) for table in tables)
            out.append(got[:k] + got[k:])
        return jnp.concatenate(out, axis=0)

    applied = apply(iterate, (own_s,))

    for f in range(faces):
        lane2[f].wait_recv()

        @pl.when(core == 0)
        def _():
            far(f, rx.at[3 * faces + f]).start()

    for f in range(faces):
        near(f, tx.at[f]).wait_recv()
        far(f, tx.at[f]).wait_recv()

    weight_rows = []
    for f in range(faces):
        lent_weight = unpack_lent(rx[meta[f]], lent_s.at[f])
        weight_rows.append(own_weights[f] + lent_weight)
    weight = jnp.concatenate([jnp.broadcast_to(w, (k, n)) for w in weight_rows], axis=0)

    rows = faces * k
    lane_face = iota((rows, rows), 1) // k
    same_face = iota((rows, rows), 0) // k == lane_face
    side = (k, rows)
    row_at, lane_at = iota(side, 0), iota(side, 1)
    lane_base = lane_at // k * k

    def orthonormal(applied, image):
        gram = jnp.where(same_face, dot(applied, image, 1, 1, HIGHEST), 0.0)
        gram = sum(face_rows(gram, f) for f in range(faces))
        inverse = jnp.where(row_at == lane_at - lane_base, 1.0, 0.0)
        pivots = jnp.ones(side, F32)
        for j in range(k):
            column = jnp.take_along_axis(gram, lane_base + j, axis=1, mode="promise_in_bounds")
            pivot = column[j : j + 1]
            factor = jnp.where(row_at > j, column / pivot, 0.0)
            pivots = jnp.where(row_at == j, pivot, pivots)
            gram = gram - factor * gram[j : j + 1]
            inverse = inverse - factor * inverse[j : j + 1]
        inverse = inverse * lax.rsqrt(pivots)
        spread = jnp.where(same_face, jnp.concatenate([inverse] * faces, axis=0), 0.0)
        return dot(spread, image, 1, 0, HIGHEST)

    for sweep in range(ITERS):
        if sweep == 0:
            applied = applied + apply(iterate, (lent_s,))
        else:
            applied = apply(iterate, (own_s, lent_s))
        image = applied / weight
        iterate = orthonormal(applied, image)

    face_of_row = iota((rows, 1), 0) // k
    counts = jnp.zeros((rows, 1), jnp.int32)
    for f in range(faces):
        counts = jnp.where(face_of_row == f, meta[faces + f], counts)
    kept_row = iota((rows, 1), 0) - face_of_row * k < counts
    basis_rows = jnp.where(kept_row, iterate, 0.0)
    for p in range(parts):
        basis_tx[p] = basis_rows[:, p * width : (p + 1) * width].reshape(faces, k, width)
    basis_copies = []
    for dp in range(1, parts):
        p = lax.rem(part + dp, parts)
        basis_copies.append(
            remote(
                basis_tx.at[p],
                basis.at[pl.ds(part * faces, faces)],
                basis_send.at[dp - 1],
                basis_recv.at[dp - 1],
                me,
                p,
            )
        )
    for copy in basis_copies:
        copy.start()
    basis_local = pltpu.make_async_copy(
        basis_tx.at[part], basis.at[pl.ds(part * faces, faces)], x0_local_sem
    )
    basis_local.start()

    applied = apply(iterate, (own_s, lent_s))
    block = dot(iterate, applied, 1, 1, HIGHEST)
    lane_kept = iota((rows, rows), 1) - lane_face * k < counts
    block = jnp.where(same_face & kept_row & lane_kept, block, 0.0)
    per_row = rows // k
    repeat = (iota((rows, rows), 0) % k == iota((rows, rows), 1) % k).astype(F32)
    block = dot(block, repeat, 1, 0, HIGHEST)
    block = jnp.where(iota((rows, rows), 0) % per_row == lane_face, block, 0.0)
    halves = k // per_row // parts
    fold_rows = parts * faces * halves
    fold_at, from_at = iota((fold_rows, rows), 0), iota((fold_rows, rows), 1)
    wanted_row = (
        fold_at // halves % faces * k
        + (fold_at // (halves * faces) * halves + fold_at % halves) * per_row
    )
    fold = (from_at // per_row * per_row == wanted_row).astype(F32)
    folded = dot(fold, block, 1, 0, HIGHEST)
    group = faces * halves
    for p in range(parts):
        cand_tx[p] = folded[p * group : (p + 1) * group]
    source = turn * parts + part
    cand_copies = []
    for i, (dk, dp, s, p) in enumerate(peers):
        cand_copies.append(
            remote(cand_tx.at[p], cand.at[source], cand_send.at[i], cand_recv.at[i], s, p)
        )
    for copy in cand_copies:
        copy.start()
    cand[source] = cand_tx[part]

    total = 4 * parts * group
    wanted = (owners_ref[...] == me).astype(F32)
    before_at, after_at = iota((total, total), 0), iota((total, total), 1)
    before = (
        (before_at % halves == 0) & (before_at // halves < after_at // halves)
    ).astype(F32)
    rank = dot(jnp.broadcast_to(wanted, (8, total)), before, 1, 0)[0:1]
    out_rows = coarse.shape[0]
    out_at, cand_at = iota((out_rows, total), 0), iota((out_rows, total), 1)
    chosen = (wanted > 0) & (rank.astype(jnp.int32) == out_at)

    for copy in cand_copies:
        copy.wait_recv()
    candidates = cand[...].reshape(total, rows)
    for h in range(halves):
        choose = jnp.where(chosen & (cand_at % halves == h), 1.0, 0.0)
        coarse[:, h * rows : (h + 1) * rows] = dot(choose, candidates, 1, 0, HIGHEST)

    for copy in basis_copies:
        copy.wait_recv()
    basis_local.wait()
    for copy in lane1 + mid + lane2 + x0_copies + basis_copies + cand_copies:
        copy.wait_send()
    for f in range(faces):
        near(f, tx.at[f]).wait_send()
        far(f, tx.at[f]).wait_send()


def shards(
    subs,
    parts,
    own_block,
    own_coupling,
    lent_block,
    lent_coupling,
    face_list,
    eig_counts,
    owner_map,
    start_block,
):
    me = lax.axis_index("sub")
    part = lax.axis_index("face")
    faces, n, _ = own_block.shape
    held = faces * parts
    k, width = start_block.shape[1:]
    rows = faces * k
    halves = k * k // rows // parts
    group = faces * halves
    mine = lax.dynamic_slice(face_list, (me * held + part * faces, 0), (faces, 2))
    distance = (mine[:, 0] - me) % subs
    slot = (distance - 1) * faces + mine[:, 1] - part * faces
    meta = jnp.concatenate([slot, lax.dynamic_slice(eig_counts, (part * faces,), (faces,))])
    spacing = subs // 4
    owners = lax.dynamic_index_in_dim(
        owner_map.reshape(4, spacing, held), me % spacing, 1, keepdims=False
    )
    owners = jnp.repeat(owners.reshape(1, 4 * held), halves, axis=1)
    packed = (n + 16, n // 2)
    dma = pltpu.SemaphoreType.DMA
    anywhere = pl.BlockSpec(memory_space=pl.ANY)
    vmem = pl.BlockSpec(memory_space=pltpu.VMEM)
    plus = len(PLUS)
    square = pltpu.VMEM((faces, n, n), BF16)
    return pl.pallas_call(
        functools.partial(kernel, subs, parts),
        out_shape=(
            jax.ShapeDtypeStruct((held, k, width), F32),
            jax.ShapeDtypeStruct((held, k * k // parts), F32),
        ),
        in_specs=[anywhere] * 5 + [vmem, pl.BlockSpec(memory_space=pltpu.SMEM)],
        out_specs=(anywhere, vmem),
        scratch_shapes=[
            square,
            square,
            square,
            square,
            square,
            square,
            pltpu.VMEM((faces, *packed), BF16),
            pltpu.VMEM((REACH * faces, *packed), BF16),
            pltpu.VMEM((plus, *packed), BF16),
            pltpu.VMEM((parts, faces, k, width), F32),
            pltpu.VMEM((parts, faces, k, width), F32),
            pltpu.VMEM((parts, group, rows), F32),
            pltpu.VMEM((4 * parts, group, rows), F32),
            dma((4, faces)),
            dma,
            dma((faces,)),
            dma((faces,)),
            dma((plus,)),
            dma((plus,)),
            dma((faces,)),
            dma((faces,)),
            dma((faces,)),
            dma((faces,)),
            dma((faces,)),
            dma((faces,)),
            dma((parts - 1,)),
            dma((parts - 1,)),
            dma((parts - 1,)),
            dma((parts - 1,)),
            dma((4 * parts - 1,)),
            dma((4 * parts - 1,)),
        ],
        compiler_params=pltpu.CompilerParams(
            collective_id=0, has_side_effects=True, vmem_limit_bytes=48 * 1024 * 1024
        ),
    )(own_block, own_coupling, lent_block, lent_coupling, start_block, owners, meta)


def solution(mesh):
    placed = (
        P(("sub", "face"), None, None),
        P(("sub", "face"), None, None),
        P(("sub", "face"), None, None),
        P(("sub", "face"), None, None),
        P(),
        P("sub"),
        P(),
        P("sub", None, "face"),
    )
    return jax.shard_map(
        functools.partial(shards, mesh.shape["sub"], mesh.shape["face"]),
        mesh=mesh,
        in_specs=placed,
        out_specs=(P("sub", None, "face"), P("sub", "face")),
        check_vma=False,
    )
```

time: 992 us -> 79.6 us (0.08); the launches traced: 979 us -> 79.3 us
  waiting for transfers between devices: 442 us -> 0 us
  other arithmetic: 268 us -> 1.44 us
  local copies, waits for them, and re-layouts: 125 us -> 7.15 us
  Pallas kernels: 0 us -> 70 us
  matrix products: 66.2 us -> 0 us
  starting transfers between devices: 63.1 us -> 0 us
  between operations: 14.6 us -> 0.69 us
    another operation x19 -> x0, other arithmetic: 260 us -> none  [the longest x10 141 us: shards(): lower_factor = jnp.linalg.cholesky(gram_matrix)]
    all_gather x5 -> x0, waiting for transfers between devices: 170 us -> none  [the longest x4 90.1 us: full_iterate(): return lax.all_gather(piece, 'face', axis=2, tiled=True)]
    psum x3 -> x0, waiting for transfers between devices: 153 us -> none  [shards(): gram_matrix = lax.psum(partial_gram, 'face')]
    ppermute x8 -> x0, waiting for transfers between devices: 95.7 us -> none  [shifted(): return lax.ppermute(block, axis, route)]
    unnamed x18 -> x11, local copies, waits for them, and re-layouts: 88.8 us -> 5.96 us
    pallas_call x0 -> x1, Pallas kernels: none -> 70 us  [shards(): pl.pallas_call(functools.partial(kernel, subs, parts), out_shape=(jax.Sha...]
    dot_general x19 -> x0, matrix products: 62.1 us -> none  [the longest x4 34.4 us: apply_rows(): return jnp.einsum('fkm,frm->fkr', iterate, operator, precision=HIGHEST)]
    ppermute x8 -> x0, starting transfers between devices: 43.8 us -> none  [shifted(): return lax.ppermute(block, axis, route)]
  transfers between devices with their start and end apart: 21 -> 0, of which waited for: 12 -> 0; matrix products, arithmetic and copies ran while one was open for 14% -> 0% of each run, Pallas kernels for 0% -> 0%
where the time goes in v1:
time: 79.6 us; the launch traced here: 79.3 us
  Pallas kernels  70 us (88%)
  local copies, waits for them, and re-layouts  7.15 us (9%)
  other arithmetic  1.44 us (2%)
    pallas_call x1, Pallas kernels, shards(): pl.pallas_call(functools.partial(kernel, subs, parts), out_shape=(jax.Sha...  70 us
    unnamed x11, local copies, waits for them, and re-layouts  5.96 us

profile of v1, /device:TPU:1, one launch (start us, length us, event | category | flops | bytes accessed | tf_op | source)
XLA Modules:
  0.0 79.3 jit_solution(5795529966817332459)
XLA Ops:
  0.6 0.0 copy-start
  0.7 0.7 dynamic_slice.12
  1.4 0.0 copy-done
  1.4 0.1 constant_dynamic-slice_fusion
  1.5 0.1 pad_add_fusion.meta
  1.6 0.5 broadcast.28
  2.1 1.3 %reduce.3 = s32[1024]{0:T(1024)S(1)} reduce(s32[1024,1]{0,1:T(1,128)} %param.14, s32[]{:T(128)} %broadcast.28), dimensions={1}, to_apply=%param.14.reduce_sub_computation.3 | reduce | bytes 8196 | tf_op args[6]
  3.4 0.1 reshape.19
  3.5 0.1 reshape.20
  3.6 0.1 broadcast_in_dim.5
  3.7 0.1 broadcast_in_dim.6.owners_ref
  3.8 0.0 copy-start.1
  3.8 1.6 %copy-done.1 = bf16[4,512,512]{2,1,0:T(8,128)(2,1)S(1)} copy-done((bf16[4,512,512]{2,1,0:T(8,128)(2,1)S(1)}, bf16[4,512,512]{2,1,0:T(8,128)(2,1)}, u32[]{:S(2)}) %copy-start.1) | copy-done | bytes 2097176
  5.4 0.0 copy-start.2
  5.4 1.6 %copy-done.2 = bf16[4,512,512]{2,1,0:T(8,128)(2,1)S(1)} copy-done((bf16[4,512,512]{2,1,0:T(8,128)(2,1)S(1)}, bf16[4,512,512]{2,1,0:T(8,128)(2,1)}, u32[]{:S(2)}) %copy-start.2) | copy-done | bytes 2097176
  7.0 0.0 copy-start.3
  7.0 0.9 %copy-done.3 = f32[16,32,128]{2,1,0:T(8,128)S(1)} copy-done((f32[16,32,128]{2,1,0:T(8,128)S(1)}, f32[16,32,128]{2,1,0:T(8,128)}, u32[]{:S(2)}) %copy-start.3) | copy-done | bytes 262168
  8.0 70.0 %shard_map.95 = (f32[16,32,128]{2,1,0:T(8,128)S(1)}, f32[16,256]{1,0:T(8,128)S(1)}) custom-call(bf16[4,512,512]{2,1,0:T(8,128)(2,1)S(1)} %copy-done.1, bf16[4,512,512]{2,1,0:T(8,128)(2,1)S(1)} %copy-done.2, bf16[4,512,512]{2,1,0:T(8,128)(2,1)} %lent_block.1, bf16[4,512,512]{2,1,0:T(8,128)(2,1)} %lent_coupling.1, f32[16,32,128]{2,1,0:T(8,128)S(1)} %copy-done.3, ...), custom_call_target="tpu_custom_call" | custom-call | tf_op jit(solution)/shard_map/pallas_call | solution.py:443
  78.0 0.7 copy.15
  78.7 0.6 copy.16
  (2 shorter events, 0.0 us)
Async XLA Ops:
  0.6 0.8 copy-start
  3.8 1.6 %copy-start.1 = (bf16[4,512,512]{2,1,0:T(8,128)(2,1)S(1)}, bf16[4,512,512]{2,1,0:T(8,128)(2,1)}, u32[]{:S(2)}) copy-start(bf16[4,512,512]{2,1,0:T(8,128)(2,1)} %own_block.1) | copy-start | bytes 6291460
  5.4 1.6 %copy-start.2 = (bf16[4,512,512]{2,1,0:T(8,128)(2,1)S(1)}, bf16[4,512,512]{2,1,0:T(8,128)(2,1)}, u32[]{:S(2)}) copy-start(bf16[4,512,512]{2,1,0:T(8,128)(2,1)} %own_coupling.1) | copy-start | bytes 6291460
  7.0 0.9 %copy-start.3 = (f32[16,32,128]{2,1,0:T(8,128)S(1)}, f32[16,32,128]{2,1,0:T(8,128)}, u32[]{:S(2)}) copy-start(f32[16,32,128]{2,1,0:T(8,128)} %start_block.1) | copy-start | bytes 786436

commit v2 on v1

v2 whole, which is shorter than its diff:
```python
import functools

import jax
import jax.numpy as jnp
from jax import lax
from jax.experimental import pallas as pl
from jax.experimental.pallas import tpu as pltpu
from jax.sharding import PartitionSpec as P

ITERS = 3
REACH = 4
RING = 4
RELAYED = 3
DEPTH = 2
BLOCK = 8

HIGHEST = lax.Precision.HIGHEST
MESH = pl.DeviceIdType.MESH
F32 = jnp.float32
BF16 = jnp.bfloat16


def iota(shape, dim):
    return lax.broadcasted_iota(jnp.int32, shape, dim)


def dot(a, b, ca, cb, precision=None):
    return lax.dot_general(
        a, b, (((ca,), (cb,)), ((), ())), precision=precision, preferred_element_type=F32
    )


def pack_lent(block, coupling, out_ref):
    n = block.shape[0]
    h = n // 2
    c0, c1 = coupling[:, :h], coupling[:, h:]
    b00 = block[:h, :h].astype(F32)
    b11 = block[h:, h:].astype(F32)
    row, col = iota((h, h), 0), iota((h, h), 1)
    out_ref[0:h, :] = (block[:h, h:].astype(F32) - dot(c0, c1, 0, 0)).astype(BF16)
    s00 = b00 - dot(c0, c0, 0, 0)
    s11 = b11 - dot(c1, c1, 0, 0)
    out_ref[h : 2 * h, :] = jnp.where(row <= col, s00, s11).astype(BF16)
    eye = row == col
    diagonals = [jnp.sum(jnp.where(eye, v, 0.0), axis=0, keepdims=True) for v in (s11, b00, b11)]
    at = iota((16, h), 0)
    aux = jnp.where(at == 0, diagonals[0], jnp.where(at == 1, diagonals[1], diagonals[2]))
    out_ref[2 * h :, :] = aux.astype(BF16)


def unpack_upper(packed, out_ref):
    h = packed.shape[1]
    out_ref[:h, h:] = packed
    out_ref[h:, :h] = packed.T


def unpack_mixed(packed, out_ref):
    h = packed.shape[1]
    mixed = packed[:h].astype(F32)
    aux = packed[h:].astype(F32)
    flipped = mixed.T
    row, col = iota((h, h), 0), iota((h, h), 1)
    out_ref[:h, :h] = jnp.where(row <= col, mixed, flipped).astype(BF16)
    out_ref[h:, h:] = jnp.where(
        row > col, mixed, jnp.where(row < col, flipped, aux[0:1])
    ).astype(BF16)


def kernel(
    subs,
    parts,
    own_block,
    own_coupling,
    lent_block,
    lent_coupling,
    start_block,
    face_list,
    eig_counts,
    owner_map,
    basis,
    coarse,
    lent_b,
    lent_c,
    own_b,
    own_c,
    own_s,
    lent_s,
    lent_w,
    tx,
    rx,
    passing,
    x0,
    basis_tx,
    basis_rx,
    basis_out,
    cand_tx,
    cand,
    table_s,
    count_s,
    owner_v,
    load_sem,
    index_sem,
    x0_local_sem,
    out_sem,
    lane1_send,
    lane1_recv,
    mid_send,
    mid_recv,
    lane2_send,
    lane2_recv,
    near_send,
    near_recv,
    far_send,
    far_recv,
    x0_send,
    x0_recv,
    basis_send,
    basis_recv,
    cand_send,
    cand_recv,
):
    faces = own_b.shape[0]
    n = own_b.shape[1]
    k = start_block.shape[1]
    width = start_block.shape[2]
    me = lax.axis_index("sub")
    part = lax.axis_index("face")
    core = lax.rem(me, 2)
    x = lax.rem(me // 2, RING)
    line = me - 2 * x - core
    ahead = line + 2 * lax.rem(x + 1, RING) + core
    behind = line + 2 * lax.rem(x + RING - 1, RING) + core
    spacing = subs // 4
    residue = lax.rem(me, spacing)
    turn = me // spacing

    def around(s):
        return lax.rem(s + 2 * subs, subs)

    other = me + 1 - 2 * core
    down = around(me - 2)
    up = around(me + 2)
    onward = around(behind - 4)
    top = around(me + 4)
    top_core = lax.rem(top, 2)
    top_x = lax.rem(top // 2, RING)
    feeder = top - 2 * top_x + 2 * lax.rem(top_x + 1, RING)

    loads = []
    for f in range(faces):
        for a, (src, dst) in enumerate(((lent_coupling, lent_c), (lent_block, lent_b))):
            loads.append(pltpu.make_async_copy(src.at[f], dst.at[f], load_sem.at[a, f]))
    for f in range(faces):
        for a, (src, dst) in enumerate(((own_coupling, own_c), (own_block, own_b))):
            loads.append(pltpu.make_async_copy(src.at[f], dst.at[f], load_sem.at[a + 2, f]))
    for copy in loads:
        copy.start()
    x0_local = pltpu.make_async_copy(
        start_block.at[pl.ds(part * faces, faces)], x0.at[part], x0_local_sem
    )
    x0_local.start()
    indices = [
        pltpu.make_async_copy(src, dst, index_sem.at[i])
        for i, (src, dst) in enumerate(
            ((face_list, table_s), (eig_counts, count_s), (owner_map, owner_v))
        )
    ]
    for copy in indices:
        copy.start()

    def remote(src, dst, send, recv, s, p):
        return pltpu.make_async_remote_copy(
            src_ref=src,
            dst_ref=dst,
            send_sem=send,
            recv_sem=recv,
            device_id=(s, p),
            device_id_type=MESH,
        )

    barrier = pltpu.get_barrier_semaphore()
    greeted = [(s, part) for s in (down, up, ahead, behind, onward, feeder, other)]
    peers = []
    for dk in range(4):
        for dp in range(parts):
            if dk or dp:
                s = residue + spacing * lax.rem(turn + dk, 4)
                p = lax.rem(part + dp, parts)
                peers.append((dk, dp, s, p))
                greeted.append((s, p))
    for s, p in greeted:
        pl.semaphore_signal(barrier, inc=1, device_id=(s, p), device_id_type=MESH)

    x0_copies = []
    for dp in range(1, parts):
        p = lax.rem(part + dp, parts)
        x0_copies.append(
            remote(
                start_block.at[pl.ds(p * faces, faces)],
                x0.at[part],
                x0_send.at[dp - 1],
                x0_recv.at[dp - 1],
                me,
                p,
            )
        )
    h = n // 2
    chunks = [(f, c) for f in range(faces) for c in range(2)]
    spans = (pl.ds(0, h), pl.ds(h, h + 16))
    heights = (h, h + 16)

    def half(ref, slot, c):
        return ref.at[slot, spans[c]]

    lane1, mid, lane2 = [], [], []
    for i, (f, c) in enumerate(chunks):
        here, one, two = half(tx, f, c), half(rx, faces + f, c), half(rx, 3 * faces + f, c)
        lane1.append(remote(here, one, lane1_send.at[i], lane1_recv.at[i], down, part))
        if i >= RELAYED:
            m = i - RELAYED
            through = passing.at[m, pl.ds(0, heights[c])]
            mid.append(remote(here, through, mid_send.at[m], mid_recv.at[m], ahead, part))
            lane2.append(remote(through, two, lane2_send.at[i], lane2_recv.at[i], onward, part))
        else:
            lane2.append(remote(one, two, lane2_send.at[i], lane2_recv.at[i], down, part))

    def near(i, ref, slot):
        f, c = chunks[i]
        return remote(
            half(ref, slot, c), half(rx, f, c), near_send.at[i], near_recv.at[i], other, part
        )

    def far(i, slot):
        f, c = chunks[i]
        return remote(
            half(rx, slot, c),
            half(rx, 2 * faces + f, c),
            far_send.at[i],
            far_recv.at[i],
            other,
            part,
        )

    def unpack(i, reach):
        f, c = chunks[i]
        slot = (reach - 1) * faces + f
        packed = rx[slot, spans[c]]
        if c == 0:
            unpack_upper(packed, lent_s.at[slot])
        else:
            unpack_mixed(packed, lent_s.at[slot])
            aux = packed[h:].astype(F32)
            lent_w[slot] = jnp.concatenate([aux[1:2], aux[2:3]], axis=1)

    count = len(chunks)
    passed = count - RELAYED
    minus = lane1 + lane2[:RELAYED]
    minus_from = [None] * count + lane1[:RELAYED]
    plus = mid + lane2[RELAYED:]
    plus_from = [None] * passed + mid
    arrived = []

    def receive(copy):
        if not any(copy is c for c in arrived):
            arrived.append(copy)
            copy.wait_recv()

    def start_slot(t):
        for side, needs, depth in ((minus, minus_from, DEPTH), (plus, plus_from, passed)):
            if 0 <= t - depth < len(side):
                side[t - depth].wait_send()
            if depth <= t < len(side):
                if needs[t] is not None:
                    receive(needs[t])
                side[t].start()

    for f in range(faces):
        loads[2 * f].wait()
        loads[2 * f + 1].wait()
        pack_lent(lent_b[f], lent_c[f], tx.at[f])
        if f == 0:
            pl.semaphore_wait(barrier, len(greeted))
        for t in range(2 * f, min(2 * f + 2, DEPTH)):
            lane1[t].start()
        for t in range(2 * f, 2 * f + 2):
            if t >= RELAYED:
                mid[t - RELAYED].start()

        @pl.when(core == 1)
        def _():
            for i in (2 * f, 2 * f + 1):
                near(i, tx, f).start()

    for copy in x0_copies:
        copy.start()

    own_weights = []
    eye = iota((n, n), 0) == iota((n, n), 1)
    for f in range(faces):
        loads[2 * faces + 2 * f].wait()
        loads[2 * faces + 2 * f + 1].wait()
        coupling = own_c[f]
        block = own_b[f].astype(F32)
        own_s[f] = (block - dot(coupling, coupling, 0, 0)).astype(BF16)
        own_weights.append(jnp.sum(jnp.where(eye, block, 0.0), axis=0, keepdims=True))

    def split(value):
        high = value.astype(BF16)
        return high, (value - high.astype(F32)).astype(BF16)

    def face_rows(value, f):
        return value[f * k : (f + 1) * k]

    def apply(value, tables):
        high, low = split(value)
        out = []
        for f in range(faces):
            stacked = jnp.concatenate([face_rows(high, f), face_rows(low, f)], axis=0)
            got = sum(dot(stacked, table(f), 1, 0) for table in tables)
            out.append(got[:k] + got[k:])
        return jnp.concatenate(out, axis=0)

    def slot_of(copy):
        return next(t for side in (minus, plus) for t, c in enumerate(side) if c is copy)

    last = max(len(minus), len(plus))
    tasks = {}
    for i, (f, c) in enumerate(chunks):
        two = slot_of(lane2[i])
        for t, task in (
            (i + DEPTH, "one"),
            (i + DEPTH + 2, "near"),
            (two + DEPTH, "two"),
            (two + DEPTH + 2, "far"),
        ):
            tasks.setdefault(t, []).append((i, task))
    for t in range(DEPTH, last + passed + 3):
        if t < max(len(minus) + DEPTH, len(plus) + passed):
            start_slot(t)
        if t == DEPTH + 2:
            x0_local.wait()
            for copy in x0_copies:
                copy.wait_recv()
            iterate = jnp.concatenate(
                [x0[p].reshape(faces * k, width) for p in range(parts)], axis=1
            )
            applied = apply(iterate, (own_s.__getitem__,))
        for i, task in tasks.get(t, ()):
            f, c = chunks[i]
            if task == "one":
                receive(lane1[i])

                @pl.when(core == 0)
                def _():
                    near(i, rx, faces + f).start()

                @pl.when(core == 1)
                def _():
                    far(i, faces + f).start()

                unpack(i, 2)
            elif task == "near":
                near(i, tx, 0).wait_recv()
                unpack(i, 1)
            elif task == "two":
                receive(lane2[i])

                @pl.when(core == 0)
                def _():
                    far(i, 3 * faces + f).start()

                unpack(i, 4)
            else:
                far(i, 0).wait_recv()
                unpack(i, 3)

    for copy in indices:
        copy.wait()
    slots, weight_rows = [], []
    for f in range(faces):
        at = me * faces * parts + part * faces + f
        distance = lax.rem(table_s[0, at] - me + subs, subs)
        slot = (distance - 1) * faces + table_s[1, at] - part * faces
        slots.append(jnp.clip(slot, 0, REACH * faces - 1))
        weight_rows.append(own_weights[f] + lent_w[slots[f]])
    weight = jnp.concatenate([jnp.broadcast_to(w, (k, n)) for w in weight_rows], axis=0)

    def lent(f):
        return lent_s[slots[f]]

    rows = faces * k
    lane_face = iota((rows, rows), 1) // k
    same_face = iota((rows, rows), 0) // k == lane_face
    side = (k, rows)
    row_at, lane_at = iota(side, 0), iota(side, 1)
    lane_base = lane_at // k * k

    def inverse_factor(applied, image):
        gram = jnp.where(same_face, dot(applied, image, 1, 1, HIGHEST), 0.0)
        gram = sum(face_rows(gram, f) for f in range(faces))
        inverse = jnp.where(row_at == lane_at - lane_base, 1.0, 0.0)
        pivots = jnp.ones(side, F32)
        for j in range(0, k, BLOCK):
            columns = [
                jnp.take_along_axis(gram, lane_base + j + i, axis=1, mode="promise_in_bounds")
                for i in range(BLOCK)
            ]
            gram_rows = [gram[j + i : j + i + 1] for i in range(BLOCK)]
            inverse_rows = [inverse[j + i : j + i + 1] for i in range(BLOCK)]
            for i in range(BLOCK):
                at = j + i
                pivot = columns[i][at : at + 1]
                factor = jnp.where(row_at > at, columns[i] * (1.0 / pivot), 0.0)
                pivots = jnp.where(row_at == at, pivot, pivots)
                for later in range(i + 1, BLOCK):
                    columns[later] = columns[later] - factor * columns[later][at : at + 1]
                    scale = factor[j + later : j + later + 1]
                    gram_rows[later] = gram_rows[later] - scale * gram_rows[i]
                    inverse_rows[later] = inverse_rows[later] - scale * inverse_rows[i]
                gram = gram - factor * gram_rows[i]
                inverse = inverse - factor * inverse_rows[i]
        return inverse * lax.rsqrt(pivots)

    applied = applied + apply(iterate, (lent,))
    for sweep in range(ITERS):
        image = applied / weight
        applied_next = apply(image, (own_s.__getitem__, lent))
        inverse = inverse_factor(applied, image)
        repeated = jnp.concatenate([inverse] * faces, axis=0)
        spread = jnp.where(same_face, repeated, 0.0)
        if sweep < ITERS - 1:
            applied = dot(spread, applied_next, 1, 0, HIGHEST)
    iterate = dot(spread, image, 1, 0, HIGHEST)

    face_of_row = iota((rows, 1), 0) // k
    counts = jnp.zeros((rows, 1), jnp.int32)
    for f in range(faces):
        counts = jnp.where(face_of_row == f, count_s[part * faces + f], counts)
    kept_row = iota((rows, 1), 0) - face_of_row * k < counts
    basis_rows = jnp.where(kept_row, iterate, 0.0)
    for p in range(parts):
        basis_tx[p] = (
            basis_rows[:, p * width : (p + 1) * width].reshape(faces, k, width).astype(BF16)
        )
    basis_copies = []
    for dp in range(1, parts):
        p = lax.rem(part + dp, parts)
        basis_copies.append(
            remote(
                basis_tx.at[p],
                basis_rx.at[part],
                basis_send.at[dp - 1],
                basis_recv.at[dp - 1],
                me,
                p,
            )
        )
    for copy in basis_copies:
        copy.start()

    block = jnp.where(same_face, dot(image, applied_next, 1, 1, HIGHEST), 0.0)
    block = dot(spread, dot(block, repeated, 1, 1, HIGHEST), 1, 0, HIGHEST)
    lane_kept = iota((rows, rows), 1) % k < counts
    per_row = rows // k
    mine_row = iota((rows, rows), 0) % per_row == lane_face
    block = jnp.where(mine_row & kept_row & lane_kept, block, 0.0)
    halves = k // per_row // parts
    fold_rows = parts * faces * halves
    fold_at, from_at = iota((fold_rows, rows), 0), iota((fold_rows, rows), 1)
    wanted_row = (
        fold_at // halves % faces * k
        + (fold_at // (halves * faces) * halves + fold_at % halves) * per_row
    )
    fold = (from_at // per_row * per_row == wanted_row).astype(F32)
    folded = dot(fold, block, 1, 0, HIGHEST)
    group = faces * halves
    for p in range(parts):
        cand_tx[p] = folded[p * group : (p + 1) * group]
    source = turn * parts + part
    cand_copies = []
    for i, (dk, dp, s, p) in enumerate(peers):
        cand_copies.append(
            remote(cand_tx.at[p], cand.at[source], cand_send.at[i], cand_recv.at[i], s, p)
        )
    for copy in cand_copies:
        copy.start()
    cand[source] = cand_tx[part]

    total = 4 * parts * group
    held = faces * parts
    lanes = owner_v.shape[1]
    cand_of = iota(owner_v.shape, 1) // halves
    first = cand_of // held * spacing * held + residue * held
    spot = first + cand_of % held
    owners = jnp.take_along_axis(owner_v[...], spot % lanes, axis=1, mode="promise_in_bounds")
    wanted = (owners == me) & (iota(owner_v.shape, 0) == spot // lanes)
    wanted = jnp.sum(wanted.astype(F32), axis=0, keepdims=True)
    before_at, after_at = iota((total, total), 0), iota((total, total), 1)
    before = (
        (before_at % halves == 0) & (before_at // halves < after_at // halves)
    ).astype(F32)
    rank = dot(jnp.broadcast_to(wanted, (8, total)), before, 1, 0)[0:1]
    out_rows = coarse.shape[0]
    out_at, cand_at = iota((out_rows, total), 0), iota((out_rows, total), 1)
    chosen = (wanted > 0) & (rank.astype(jnp.int32) == out_at)

    basis_out[pl.ds(part * faces, faces)] = basis_tx[part].astype(F32)
    for dp in range(1, parts):
        basis_copies[dp - 1].wait_recv()
        p = lax.rem(part + parts - dp, parts)
        basis_out[pl.ds(p * faces, faces)] = basis_rx[p].astype(F32)
    out_copy = pltpu.make_async_copy(basis_out, basis, out_sem)
    out_copy.start()

    for copy in cand_copies:
        copy.wait_recv()
    candidates = cand[...].reshape(total, rows)
    for h in range(halves):
        choose = jnp.where(chosen & (cand_at % halves == h), 1.0, 0.0)
        coarse[:, h * rows : (h + 1) * rows] = dot(choose, candidates, 1, 0, HIGHEST)

    out_copy.wait()
    for copy in x0_copies + basis_copies + cand_copies:
        copy.wait_send()
    for i in range(len(chunks)):
        near(i, tx, 0).wait_send()
        far(i, 0).wait_send()


def shards(
    subs,
    parts,
    own_block,
    own_coupling,
    lent_block,
    lent_coupling,
    face_list,
    eig_counts,
    owner_map,
    start_block,
):
    faces, n, _ = own_block.shape
    held = faces * parts
    k, width = start_block.shape[1:]
    rows = faces * k
    halves = k * k // rows // parts
    group = faces * halves
    packed = (n + 16, n // 2)
    dma = pltpu.SemaphoreType.DMA
    anywhere = pl.BlockSpec(memory_space=pl.ANY)
    vmem = pl.BlockSpec(memory_space=pltpu.VMEM)
    chunks = 2 * faces
    square = pltpu.VMEM((faces, n, n), BF16)
    return pl.pallas_call(
        functools.partial(kernel, subs, parts),
        out_shape=(
            jax.ShapeDtypeStruct((held, k, width), F32),
            jax.ShapeDtypeStruct((held, k * k // parts), F32),
        ),
        in_specs=[anywhere] * 8,
        out_specs=(anywhere, vmem),
        scratch_shapes=[
            square,
            square,
            square,
            square,
            square,
            pltpu.VMEM((REACH * faces, n, n), BF16),
            pltpu.VMEM((REACH * faces, 1, n), F32),
            pltpu.VMEM((faces, *packed), BF16),
            pltpu.VMEM((REACH * faces, *packed), BF16),
            pltpu.VMEM((chunks - RELAYED, n // 2 + 16, n // 2), BF16),
            pltpu.VMEM((parts, faces, k, width), F32),
            pltpu.VMEM((parts, faces, k, width), BF16),
            pltpu.VMEM((parts, faces, k, width), BF16),
            pltpu.VMEM((held, k, width), F32),
            pltpu.VMEM((parts, group, rows), F32),
            pltpu.VMEM((4 * parts, group, rows), F32),
            pltpu.SMEM((2, held * subs), jnp.int32),
            pltpu.SMEM((held,), jnp.int32),
            pltpu.VMEM((held * subs // rows, rows), jnp.int32),
            dma((4, faces)),
            dma((3,)),
            dma,
            dma,
            dma((chunks,)),
            dma((chunks,)),
            dma((chunks - RELAYED,)),
            dma((chunks - RELAYED,)),
            dma((chunks,)),
            dma((chunks,)),
            dma((chunks,)),
            dma((chunks,)),
            dma((chunks,)),
            dma((chunks,)),
            dma((parts - 1,)),
            dma((parts - 1,)),
            dma((parts - 1,)),
            dma((parts - 1,)),
            dma((4 * parts - 1,)),
            dma((4 * parts - 1,)),
        ],
        compiler_params=pltpu.CompilerParams(
            collective_id=0, has_side_effects=True, vmem_limit_bytes=60 * 1024 * 1024
        ),
    )(
        own_block,
        own_coupling,
        lent_block,
        lent_coupling,
        start_block,
        face_list.T,
        eig_counts,
        owner_map.reshape(held * subs // rows, rows),
    )


def solution(mesh):
    placed = (
        P(("sub", "face"), None, None),
        P(("sub", "face"), None, None),
        P(("sub", "face"), None, None),
        P(("sub", "face"), None, None),
        P(),
        P("sub"),
        P(),
        P("sub", None, "face"),
    )
    return jax.shard_map(
        functools.partial(shards, mesh.shape["sub"], mesh.shape["face"]),
        mesh=mesh,
        in_specs=placed,
        out_specs=(P("sub", None, "face"), P("sub", "face")),
        check_vma=False,
    )
```

time: 79.6 us -> 66.4 us (0.83)
  Pallas kernels: 70 us -> 62.6 us
  local copies, waits for them, and re-layouts: 7.15 us -> 2.99 us
  other arithmetic: 1.44 us -> 0 us
    pallas_call x1, Pallas kernels: 70 us -> 62.6 us  [shards(): pl.pallas_call(functools.partial(kernel, subs, parts), out_shape=(jax.Sha...]
    unnamed x11 -> x2, local copies, waits for them, and re-layouts: 5.96 us -> 2.99 us
    unnamed x1 -> x0, other arithmetic: 1.35 us -> none
    dynamic_slice x3 -> x0, local copies, waits for them, and re-layouts: 0.81 us -> none  [the longest x1 0.73 us: shards(): lax.dynamic_slice(eig_counts, (part * faces,), (faces,))]
where the time goes in v2:
time: 66.4 us; the launch traced here: 66.2 us
  Pallas kernels  62.6 us (94%)
  local copies, waits for them, and re-layouts  2.99 us (5%)
    pallas_call x1, Pallas kernels, shards(): pl.pallas_call(functools.partial(kernel, subs, parts), out_shape=(jax.Sha...  62.6 us
    unnamed x2, local copies, waits for them, and re-layouts  2.99 us

profile of v2, /device:TPU:1, one launch (start us, length us, event | category | flops | bytes accessed | tf_op | source)
XLA Modules:
  0.0 66.2 jit_solution(12823760050934083123)
XLA Ops:
  0.6 62.6 %shard_map.95 = (f32[16,32,128]{2,1,0:T(8,128)}, f32[16,256]{1,0:T(8,128)}) custom-call(bf16[4,512,512]{2,1,0:T(8,128)(2,1)} %own_block.1, bf16[4,512,512]{2,1,0:T(8,128)(2,1)} %own_coupling.1, bf16[4,512,512]{2,1,0:T(8,128)(2,1)} %lent_block.1, bf16[4,512,512]{2,1,0:T(8,128)(2,1)} %lent_coupling.1, f32[16,32,128]{2,1,0:T(8,128)} %start_block.1, ...), custom_call_target="tpu_custom_call" | custom-call | tf_op jit(solution)/shard_map/pallas_call | solution.py:554
  63.2 1.7 %copy.12 = f32[16,32,128]{2,1,0:T(8,128)} copy(f32[16,32,128]{2,1,0:T(8,128)} %get-tuple-element.4) | data formatting | bytes 524288
  64.9 1.3 %copy.13 = f32[16,256]{1,0:T(8,128)} copy(f32[16,256]{1,0:T(8,128)} %get-tuple-element.5) | data formatting | bytes 32768

commit v3 on v2

--- a/solution.py
+++ b/solution.py
@@ -30,14 +30,18 @@
     )
 
 
-def pack_lent(block, coupling, out_ref):
-    n = block.shape[0]
-    h = n // 2
+def pack_upper(block, coupling, out_ref):
+    h = block.shape[0] // 2
+    product = dot(coupling[:, :h], coupling[:, h:], 0, 0)
+    out_ref[0:h, :] = (block[:h, h:].astype(F32) - product).astype(BF16)
+
+
+def pack_mixed(block, coupling, out_ref):
+    h = block.shape[0] // 2
     c0, c1 = coupling[:, :h], coupling[:, h:]
     b00 = block[:h, :h].astype(F32)
     b11 = block[h:, h:].astype(F32)
     row, col = iota((h, h), 0), iota((h, h), 1)
-    out_ref[0:h, :] = (block[:h, h:].astype(F32) - dot(c0, c1, 0, 0)).astype(BF16)
     s00 = b00 - dot(c0, c0, 0, 0)
     s11 = b11 - dot(c1, c1, 0, 0)
     out_ref[h : 2 * h, :] = jnp.where(row <= col, s00, s11).astype(BF16)
@@ -77,8 +81,9 @@
     face_list,
     eig_counts,
     owner_map,
-    basis,
-    coarse,
+    basis_rx,
+    cand,
+    choose_out,
     lent_b,
     lent_c,
     own_b,
@@ -91,10 +96,8 @@
     passing,
     x0,
     basis_tx,
-    basis_rx,
-    basis_out,
+    block_v,
     cand_tx,
-    cand,
     table_s,
     count_s,
     owner_v,
@@ -153,20 +156,17 @@
     for f in range(faces):
         for a, (src, dst) in enumerate(((own_coupling, own_c), (own_block, own_b))):
             loads.append(pltpu.make_async_copy(src.at[f], dst.at[f], load_sem.at[a + 2, f]))
-    for copy in loads:
+    for copy in loads[:2]:
         copy.start()
     x0_local = pltpu.make_async_copy(
         start_block.at[pl.ds(part * faces, faces)], x0.at[part], x0_local_sem
     )
-    x0_local.start()
     indices = [
         pltpu.make_async_copy(src, dst, index_sem.at[i])
         for i, (src, dst) in enumerate(
             ((face_list, table_s), (eig_counts, count_s), (owner_map, owner_v))
         )
     ]
-    for copy in indices:
-        copy.start()
 
     def remote(src, dst, send, recv, s, p):
         return pltpu.make_async_remote_copy(
@@ -274,22 +274,25 @@
                     receive(needs[t])
                 side[t].start()
 
+    def start_half(i):
+        if i < DEPTH:
+            lane1[i].start()
+        if i >= RELAYED:
+            mid[i - RELAYED].start()
+
+    later = (loads[2:6], loads[6:10] + indices, loads[10:13], loads[13:16] + [x0_local])
     for f in range(faces):
         loads[2 * f].wait()
         loads[2 * f + 1].wait()
-        pack_lent(lent_b[f], lent_c[f], tx.at[f])
+        for copy in later[f]:
+            copy.start()
+        block, coupling = lent_b[f], lent_c[f]
+        pack_upper(block, coupling, tx.at[f])
         if f == 0:
             pl.semaphore_wait(barrier, len(greeted))
-        for t in range(2 * f, min(2 * f + 2, DEPTH)):
-            lane1[t].start()
-        for t in range(2 * f, 2 * f + 2):
-            if t >= RELAYED:
-                mid[t - RELAYED].start()
-
-        @pl.when(core == 1)
-        def _():
-            for i in (2 * f, 2 * f + 1):
-                near(i, tx, f).start()
+        start_half(2 * f)
+        pack_mixed(block, coupling, tx.at[f])
+        start_half(2 * f + 1)
 
     for copy in x0_copies:
         copy.start()
@@ -356,6 +359,7 @@
 
                 @pl.when(core == 1)
                 def _():
+                    near(i, tx, f).start()
                     far(i, faces + f).start()
 
                 unpack(i, 2)
@@ -464,18 +468,14 @@
     per_row = rows // k
     mine_row = iota((rows, rows), 0) % per_row == lane_face
     block = jnp.where(mine_row & kept_row & lane_kept, block, 0.0)
+    block_v[...] = block
+    folded = sum(block_v[pl.ds(i, k, stride=per_row), :] for i in range(per_row))
     halves = k // per_row // parts
-    fold_rows = parts * faces * halves
-    fold_at, from_at = iota((fold_rows, rows), 0), iota((fold_rows, rows), 1)
-    wanted_row = (
-        fold_at // halves % faces * k
-        + (fold_at // (halves * faces) * halves + fold_at % halves) * per_row
-    )
-    fold = (from_at // per_row * per_row == wanted_row).astype(F32)
-    folded = dot(fold, block, 1, 0, HIGHEST)
     group = faces * halves
     for p in range(parts):
-        cand_tx[p] = folded[p * group : (p + 1) * group]
+        for f in range(faces):
+            at = f * k // per_row + p * halves
+            cand_tx[p, f * halves : (f + 1) * halves] = folded[at : at + halves]
     source = turn * parts + part
     cand_copies = []
     for i, (dk, dp, s, p) in enumerate(peers):
@@ -484,7 +484,12 @@
         )
     for copy in cand_copies:
         copy.start()
-    cand[source] = cand_tx[part]
+    own_copies = [
+        pltpu.make_async_copy(basis_tx.at[part], basis_rx.at[part], out_sem.at[0]),
+        pltpu.make_async_copy(cand_tx.at[part], cand.at[source], out_sem.at[1]),
+    ]
+    for copy in own_copies:
+        copy.start()
 
     total = 4 * parts * group
     held = faces * parts
@@ -500,31 +505,31 @@
         (before_at % halves == 0) & (before_at // halves < after_at // halves)
     ).astype(F32)
     rank = dot(jnp.broadcast_to(wanted, (8, total)), before, 1, 0)[0:1]
-    out_rows = coarse.shape[0]
+    out_rows = held
     out_at, cand_at = iota((out_rows, total), 0), iota((out_rows, total), 1)
     chosen = (wanted > 0) & (rank.astype(jnp.int32) == out_at)
 
-    basis_out[pl.ds(part * faces, faces)] = basis_tx[part].astype(F32)
-    for dp in range(1, parts):
-        basis_copies[dp - 1].wait_recv()
-        p = lax.rem(part + parts - dp, parts)
-        basis_out[pl.ds(p * faces, faces)] = basis_rx[p].astype(F32)
-    out_copy = pltpu.make_async_copy(basis_out, basis, out_sem)
-    out_copy.start()
-
-    for copy in cand_copies:
+    choose = [jnp.where(chosen & (cand_at % halves == h), 1.0, 0.0) for h in range(halves)]
+    choose_out[...] = jnp.concatenate(choose, axis=0)
+
+    for copy in basis_copies + cand_copies:
         copy.wait_recv()
-    candidates = cand[...].reshape(total, rows)
-    for h in range(halves):
-        choose = jnp.where(chosen & (cand_at % halves == h), 1.0, 0.0)
-        coarse[:, h * rows : (h + 1) * rows] = dot(choose, candidates, 1, 0, HIGHEST)
-
-    out_copy.wait()
+    for copy in own_copies:
+        copy.wait()
     for copy in x0_copies + basis_copies + cand_copies:
         copy.wait_send()
     for i in range(len(chunks)):
         near(i, tx, 0).wait_send()
         far(i, 0).wait_send()
+
+
+def finish(basis_rx, cand, choose, basis, coarse):
+    basis[...] = basis_rx[...].reshape(basis.shape).astype(F32)
+    rows = coarse.shape[0]
+    lanes = cand.shape[2]
+    placed = dot(choose[...], cand[...].reshape(choose.shape[1], lanes), 1, 0, HIGHEST)
+    for h in range(coarse.shape[1] // lanes):
+        coarse[:, h * lanes : (h + 1) * lanes] = placed[h * rows : (h + 1) * rows]
 
 
 def shards(
@@ -551,14 +556,15 @@
     vmem = pl.BlockSpec(memory_space=pltpu.VMEM)
     chunks = 2 * faces
     square = pltpu.VMEM((faces, n, n), BF16)
-    return pl.pallas_call(
+    arrived = pl.pallas_call(
         functools.partial(kernel, subs, parts),
         out_shape=(
-            jax.ShapeDtypeStruct((held, k, width), F32),
-            jax.ShapeDtypeStruct((held, k * k // parts), F32),
+            jax.ShapeDtypeStruct((parts, faces, k, width), BF16),
+            jax.ShapeDtypeStruct((4 * parts, group, rows), F32),
+            jax.ShapeDtypeStruct((held * halves, 4 * parts * group), F32),
         ),
         in_specs=[anywhere] * 8,
-        out_specs=(anywhere, vmem),
+        out_specs=(anywhere, anywhere, vmem),
         scratch_shapes=[
             square,
             square,
@@ -572,17 +578,15 @@
             pltpu.VMEM((chunks - RELAYED, n // 2 + 16, n // 2), BF16),
             pltpu.VMEM((parts, faces, k, width), F32),
             pltpu.VMEM((parts, faces, k, width), BF16),
-            pltpu.VMEM((parts, faces, k, width), BF16),
-            pltpu.VMEM((held, k, width), F32),
+            pltpu.VMEM((rows, rows), F32),
             pltpu.VMEM((parts, group, rows), F32),
-            pltpu.VMEM((4 * parts, group, rows), F32),
             pltpu.SMEM((2, held * subs), jnp.int32),
             pltpu.SMEM((held,), jnp.int32),
             pltpu.VMEM((held * subs // rows, rows), jnp.int32),
             dma((4, faces)),
             dma((3,)),
             dma,
-            dma,
+            dma((2,)),
             dma((chunks,)),
             dma((chunks,)),
             dma((chunks - RELAYED,)),
@@ -613,6 +617,13 @@
         eig_counts,
         owner_map.reshape(held * subs // rows, rows),
     )
+    return pl.pallas_call(
+        finish,
+        out_shape=(
+            jax.ShapeDtypeStruct((held, k, width), F32),
+            jax.ShapeDtypeStruct((held, k * k // parts), F32),
+        ),
+    )(*arrived)
 
 
 def solution(mesh):

time: 66.4 us -> 65.1 us (0.980)
  local copies, waits for them, and re-layouts: 2.99 us -> 0 us
  Pallas kernels: 62.6 us -> 64.3 us
    unnamed x2 -> x0, local copies, waits for them, and re-layouts: 2.99 us -> none
    pallas_call x0 -> x1, Pallas kernels: none -> 1.72 us  [shards(): pl.pallas_call(finish, out_shape=(jax.ShapeDtypeStruct((held, k, width),...]
where the time goes in v3:
time: 65.1 us; the launch traced here: 65 us
  Pallas kernels  64.3 us (99%)
    pallas_call x1, Pallas kernels, shards(): pl.pallas_call(functools.partial(kernel, subs, parts), out_shape=(jax.Sha...  62.6 us
    pallas_call x1, Pallas kernels, shards(): pl.pallas_call(finish, out_shape=(jax.ShapeDtypeStruct((held, k, width),...  1.72 us

profile of v3, /device:TPU:1, one launch (start us, length us, event | category | flops | bytes accessed | tf_op | source)
XLA Modules:
  0.0 65.0 jit_solution(2303715537399284618)
XLA Ops:
  0.6 62.6 %shard_map.95 = (bf16[4,4,32,128]{3,2,1,0:T(8,128)(2,1)}, f32[16,8,128]{2,1,0:T(8,128)}, f32[32,128]{1,0:T(8,128)}) custom-call(bf16[4,512,512]{2,1,0:T(8,128)(2,1)} %own_block.1, bf16[4,512,512]{2,1,0:T(8,128)(2,1)} %own_coupling.1, bf16[4,512,512]{2,1,0:T(8,128)(2,1)} %lent_block.1, bf16[4,512,512]{2,1,0:T(8,128)(2,1)} %lent_coupling.1, ...), custom_call_target="tpu_custom_call" | custom-call | tf_op jit(solution)/shard_map/pallas_call | solution.py:559
  63.3 1.7 %shard_map.96 = (f32[16,32,128]{2,1,0:T(8,128)}, f32[16,256]{1,0:T(8,128)}) custom-call(bf16[4,4,32,128]{3,2,1,0:T(8,128)(2,1)} %get-tuple-element.5.basis_rx, f32[16,8,128]{2,1,0:T(8,128)} %get-tuple-element.6.cand, f32[32,128]{1,0:T(8,128)} %get-tuple-element.7.choose), custom_call_target="tpu_custom_call" | custom-call | tf_op jit(solution)/shard_map/pallas_call | solution.py:620

commit v4 on v3

--- a/solution.py
+++ b/solution.py
@@ -28,6 +28,16 @@
     return lax.dot_general(
         a, b, (((ca,), (cb,)), ((), ())), precision=precision, preferred_element_type=F32
     )
+
+
+def split(value):
+    high = value.astype(BF16)
+    return high, (value - high.astype(F32)).astype(BF16)
+
+
+def dot3(a, b, ca, cb):
+    (ah, al), (bh, bl) = split(a), split(b)
+    return dot(ah, bh, ca, cb) + (dot(ah, bl, ca, cb) + dot(al, bh, ca, cb))
 
 
 def pack_upper(block, coupling, out_ref):
@@ -307,10 +317,6 @@
         own_s[f] = (block - dot(coupling, coupling, 0, 0)).astype(BF16)
         own_weights.append(jnp.sum(jnp.where(eye, block, 0.0), axis=0, keepdims=True))
 
-    def split(value):
-        high = value.astype(BF16)
-        return high, (value - high.astype(F32)).astype(BF16)
-
     def face_rows(value, f):
         return value[f * k : (f + 1) * k]
 
@@ -399,8 +405,8 @@
     row_at, lane_at = iota(side, 0), iota(side, 1)
     lane_base = lane_at // k * k
 
-    def inverse_factor(applied, image):
-        gram = jnp.where(same_face, dot(applied, image, 1, 1, HIGHEST), 0.0)
+    def inverse_factor(gram):
+        gram = jnp.where(same_face, gram, 0.0)
         gram = sum(face_rows(gram, f) for f in range(faces))
         inverse = jnp.where(row_at == lane_at - lane_base, 1.0, 0.0)
         pivots = jnp.ones(side, F32)
@@ -428,13 +434,17 @@
     applied = applied + apply(iterate, (lent,))
     for sweep in range(ITERS):
         image = applied / weight
+        if sweep < ITERS - 1:
+            gram = dot3(applied, image, 1, 1)
+        else:
+            gram = dot(applied, image, 1, 1, HIGHEST)
+        inverse = inverse_factor(gram)
         applied_next = apply(image, (own_s.__getitem__, lent))
-        inverse = inverse_factor(applied, image)
         repeated = jnp.concatenate([inverse] * faces, axis=0)
         spread = jnp.where(same_face, repeated, 0.0)
         if sweep < ITERS - 1:
-            applied = dot(spread, applied_next, 1, 0, HIGHEST)
-    iterate = dot(spread, image, 1, 0, HIGHEST)
+            applied = dot3(spread, applied_next, 1, 0)
+    iterate = dot3(spread, image, 1, 0)
 
     face_of_row = iota((rows, 1), 0) // k
     counts = jnp.zeros((rows, 1), jnp.int32)
@@ -463,7 +473,7 @@
         copy.start()
 
     block = jnp.where(same_face, dot(image, applied_next, 1, 1, HIGHEST), 0.0)
-    block = dot(spread, dot(block, repeated, 1, 1, HIGHEST), 1, 0, HIGHEST)
+    block = dot3(spread, dot3(block, repeated, 1, 1), 1, 0)
     lane_kept = iota((rows, rows), 1) % k < counts
     per_row = rows // k
     mine_row = iota((rows, rows), 0) % per_row == lane_face

time: 65.1 us -> 61.8 us (0.949)
  Pallas kernels: 64.3 us -> 61.1 us
    pallas_call x1, Pallas kernels: 62.6 us -> 59.3 us  [shards(): pl.pallas_call(functools.partial(kernel, subs, parts), out_shape=(jax.Sha...]
where the time goes in v4:
time: 61.8 us; the launch traced here: 61.7 us
  Pallas kernels  61.1 us (99%)
  between operations  0.64 us (1%)
    pallas_call x1, Pallas kernels, shards(): pl.pallas_call(functools.partial(kernel, subs, parts), out_shape=(jax.Sha...  59.3 us
    pallas_call x1, Pallas kernels, shards(): pl.pallas_call(finish, out_shape=(jax.ShapeDtypeStruct((held, k, width),...  1.72 us

profile of v4, /device:TPU:1, one launch (start us, length us, event | category | flops | bytes accessed | tf_op | source)
XLA Modules:
  0.0 61.7 jit_solution(5798928694440674635)
XLA Ops:
  0.6 59.3 %shard_map.95 = (bf16[4,4,32,128]{3,2,1,0:T(8,128)(2,1)}, f32[16,8,128]{2,1,0:T(8,128)}, f32[32,128]{1,0:T(8,128)}) custom-call(bf16[4,512,512]{2,1,0:T(8,128)(2,1)} %own_block.1, bf16[4,512,512]{2,1,0:T(8,128)(2,1)} %own_coupling.1, bf16[4,512,512]{2,1,0:T(8,128)(2,1)} %lent_block.1, bf16[4,512,512]{2,1,0:T(8,128)(2,1)} %lent_coupling.1, ...), custom_call_target="tpu_custom_call" | custom-call | tf_op jit(solution)/shard_map/pallas_call | solution.py:569
  60.0 1.7 %shard_map.96 = (f32[16,32,128]{2,1,0:T(8,128)}, f32[16,256]{1,0:T(8,128)}) custom-call(bf16[4,4,32,128]{3,2,1,0:T(8,128)(2,1)} %get-tuple-element.5.basis_rx, f32[16,8,128]{2,1,0:T(8,128)} %get-tuple-element.6.cand, f32[32,128]{1,0:T(8,128)} %get-tuple-element.7.choose), custom_call_target="tpu_custom_call" | custom-call | tf_op jit(solution)/shard_map/pallas_call | solution.py:630

commit v5 on v4

--- a/solution.py
+++ b/solution.py
@@ -393,7 +393,7 @@
         slot = (distance - 1) * faces + table_s[1, at] - part * faces
         slots.append(jnp.clip(slot, 0, REACH * faces - 1))
         weight_rows.append(own_weights[f] + lent_w[slots[f]])
-    weight = jnp.concatenate([jnp.broadcast_to(w, (k, n)) for w in weight_rows], axis=0)
+    scale = jnp.concatenate([jnp.broadcast_to(1.0 / w, (k, n)) for w in weight_rows], axis=0)
 
     def lent(f):
         return lent_s[slots[f]]
@@ -433,7 +433,7 @@
 
     applied = applied + apply(iterate, (lent,))
     for sweep in range(ITERS):
-        image = applied / weight
+        image = applied * scale
         if sweep < ITERS - 1:
             gram = dot3(applied, image, 1, 1)
         else:
@@ -472,7 +472,7 @@
     for copy in basis_copies:
         copy.start()
 
-    block = jnp.where(same_face, dot(image, applied_next, 1, 1, HIGHEST), 0.0)
+    block = jnp.where(same_face, dot3(image, applied_next, 1, 1), 0.0)
     block = dot3(spread, dot3(block, repeated, 1, 1), 1, 0)
     lane_kept = iota((rows, rows), 1) % k < counts
     per_row = rows // k
@@ -537,7 +537,9 @@
     basis[...] = basis_rx[...].reshape(basis.shape).astype(F32)
     rows = coarse.shape[0]
     lanes = cand.shape[2]
-    placed = dot(choose[...], cand[...].reshape(choose.shape[1], lanes), 1, 0, HIGHEST)
+    high, low = split(cand[...].reshape(choose.shape[1], lanes))
+    picked = choose[...].astype(BF16)
+    placed = dot(picked, high, 1, 0) + dot(picked, low, 1, 0)
     for h in range(coarse.shape[1] // lanes):
         coarse[:, h * lanes : (h + 1) * lanes] = placed[h * rows : (h + 1) * rows]
 

time: 61.8 us -> 61.8 us (level)
  no operation moved by 1% of the time
where the time goes in v5:
time: 61.8 us; the launch traced here: 61.7 us
  Pallas kernels  61.1 us (99%)
  between operations  0.64 us (1%)
    pallas_call x1, Pallas kernels, shards(): pl.pallas_call(functools.partial(kernel, subs, parts), out_shape=(jax.Sha...  59.4 us
    pallas_call x1, Pallas kernels, shards(): pl.pallas_call(finish, out_shape=(jax.ShapeDtypeStruct((held, k, width),...  1.69 us

profile of v5, /device:TPU:1, one launch (start us, length us, event | category | flops | bytes accessed | tf_op | source)
XLA Modules:
  0.0 61.7 jit_solution(8304114859719294840)
XLA Ops:
  0.6 59.4 %shard_map.95 = (bf16[4,4,32,128]{3,2,1,0:T(8,128)(2,1)}, f32[16,8,128]{2,1,0:T(8,128)}, f32[32,128]{1,0:T(8,128)}) custom-call(bf16[4,512,512]{2,1,0:T(8,128)(2,1)} %own_block.1, bf16[4,512,512]{2,1,0:T(8,128)(2,1)} %own_coupling.1, bf16[4,512,512]{2,1,0:T(8,128)(2,1)} %lent_block.1, bf16[4,512,512]{2,1,0:T(8,128)(2,1)} %lent_coupling.1, ...), custom_call_target="tpu_custom_call" | custom-call | tf_op jit(solution)/shard_map/pallas_call | solution.py:571
  60.0 1.7 %shard_map.96 = (f32[16,32,128]{2,1,0:T(8,128)}, f32[16,256]{1,0:T(8,128)}) custom-call(bf16[4,4,32,128]{3,2,1,0:T(8,128)(2,1)} %get-tuple-element.5.basis_rx, f32[16,8,128]{2,1,0:T(8,128)} %get-tuple-element.6.cand, f32[32,128]{1,0:T(8,128)} %get-tuple-element.7.choose), custom_call_target="tpu_custom_call" | custom-call | tf_op jit(solution)/shard_map/pallas_call | solution.py:632
